TPU v7x, 32 devices: a whole 2x2x4 slice. The times are simulated.
32 devices in a mesh: parts: 2 (over y), seq: 4 (over x, core), blk: 4 (over z).
Axes of the slice: x: 2, y: 2, z: 4, core: 2. Of those that a mesh axis runs over, the one named last changes fastest.
Arguments:
- queries: bfloat16 [16384, 1024], P(('parts', 'seq', 'blk')), parts along dimension 0, may hold values from -6 to 6
- keyvals: bfloat16 [2, 16384, 1024], P(None, ('parts', 'seq', 'blk')), parts along dimension 1, may hold values from -6 to 6
- key_lists: int32 [128, 12], P(('parts', 'seq', 'blk')), parts along dimension 0, may hold values from 0 to 63, as said below
- live_counts: int32 [128], P(('parts', 'seq', 'blk')), parts along dimension 0, may hold values from 4 to 12, as said below
Outputs:
- attended: bfloat16 [16384, 1024], P(('parts', 'seq', 'blk')), parts along dimension 0
There are 2 independent parts, one for each index of `parts`. A program takes and returns all parts, laid end to end along the dimension named above; each array names one. Nothing has to cross between parts.
Inputs may be any that keep to these rules, and one draw needn't show every extreme that they name: `key_lists`: entry 0 of every list is the query block itself; the first live_counts entries of a list are distinct blocks at most 6 blocks from the query block; later entries are ignored. `live_counts`: number of used entries of each query block's key list.
All inputs are finite; a program needn't handle non-finite values.
Results may differ from a plain program's by a relative error of at most 0.0046.
Values may be sent and summed in bfloat16 or wider, within the bound.
A program may use at most 128 MiB of HBM per device.

v0:
```python
from functools import partial

import jax
import jax.numpy as jnp
from jax import lax
from jax.sharding import PartitionSpec as P

HEADS = 8
HEAD_DIM = 128
BLOCK = 128
REACH = 6


def from_behind(block, axis, distance):
    devices = range(lax.axis_size(axis))
    route = [(i - distance, i) for i in devices if i - distance in devices]
    return lax.ppermute(block, axis, route)


def padded(cells, sides, width):
    for axis, dim in sides:
        count = lax.axis_size(axis)
        ends = count - 1
        head = lax.slice_in_dim(cells, 0, width, axis=dim)
        tail = lax.slice_in_dim(cells, cells.shape[dim] - width, cells.shape[dim], axis=dim)
        cells = jnp.concatenate(
            [
                lax.ppermute(tail, axis, [(i, (i + 1) % count) for i in range(ends)]),
                cells,
                lax.ppermute(head, axis, [((i + 1) % count, i) for i in range(ends)]),
            ],
            axis=dim,
        )
    return cells


def masked_block(score_scale, key_rows_all, value_rows_all, block_item):
    query_block, chosen, live_count = block_item
    list_length = chosen.shape[0]
    key_rows = key_rows_all[chosen].reshape(list_length * BLOCK, HEADS, HEAD_DIM)
    value_rows = value_rows_all[chosen].reshape(list_length * BLOCK, HEADS, HEAD_DIM)
    scores = (
        jnp.einsum("qhd,khd->hqk", query_block, key_rows, preferred_element_type=jnp.float32)
        * score_scale
    )
    live_mask = jnp.arange(list_length * BLOCK, dtype=jnp.int32) // BLOCK < live_count
    scores = jnp.where(live_mask[None, None, :], scores, -jnp.inf)
    row_peak = jnp.max(scores, axis=2, keepdims=True)
    weights = jnp.exp(scores - row_peak)
    row_total = jnp.sum(weights, axis=2)
    rounded = weights.astype(jnp.bfloat16)
    summed = jnp.einsum("hqk,khd->qhd", rounded, value_rows, preferred_element_type=jnp.float32)
    result = summed / jnp.transpose(row_total)[:, :, None]
    return result.astype(jnp.bfloat16).reshape(BLOCK, HEADS * HEAD_DIM)


def fetch_direct(panel_source, offset):
    return from_behind(panel_source, ("seq", "blk"), -offset)


def on_device(queries, keyvals, key_lists, live_counts):
    local_rows = queries.shape[0]
    feature_width = queries.shape[1]
    blocks_here = local_rows // BLOCK
    reach_dev = (REACH + blocks_here - 1) // blocks_here
    joined = padded(keyvals, ((("seq", "blk"), 1),), local_rows)
    panels = {-1: joined[:, :local_rows], 0: keyvals, 1: joined[:, 2 * local_rows :]}
    far_offsets = []
    far_offsets.append(2)
    far_offsets.append(-2)
    for offset in far_offsets:
        panels[offset] = fetch_direct(keyvals, offset)
    window = jnp.concatenate(
        [panels[offset] for offset in range(-reach_dev, reach_dev + 1)], axis=1
    )
    window_blocks = window.reshape(2, (2 * reach_dev + 1) * blocks_here, BLOCK, HEADS, HEAD_DIM)
    first_block = (lax.axis_index(("seq", "blk")) - reach_dev) * blocks_here
    local_lists = key_lists - first_block
    query_blocks = queries.reshape(blocks_here, BLOCK, HEADS, HEAD_DIM)
    score_scale = HEAD_DIM ** (-0.5)
    attend_block = partial(masked_block, score_scale, window_blocks[0], window_blocks[1])
    attended = lax.map(attend_block, (query_blocks, local_lists, live_counts))
    return attended.reshape(local_rows, feature_width)


def solution(mesh):
    return jax.shard_map(
        on_device,
        mesh=mesh,
        in_specs=(
            P(("parts", "seq", "blk"), None),
            P(None, ("parts", "seq", "blk"), None),
            P(("parts", "seq", "blk"), None),
            P(("parts", "seq", "blk")),
        ),
        out_specs=P(("parts", "seq", "blk"), None),
        check_vma=False,
    )
```

profile of v0, /device:TPU:16, one launch (start us, length us, event | category | flops | bytes accessed | tf_op | source)
XLA Modules:
  0.0 378.1 jit_solution(15950168881879830485)
XLA Ops:
  0.0 2.0 collective-permute-start
  2.1 3.5 collective-permute-start.1
  5.5 4.7 %collective-permute-start.2 = (bf16[2,512,1024]{2,1,0:T(8,128)(2,1)}, bf16[2,512,1024]{2,1,0:T(8,128)(2,1)}, u32[]{:S(2)}, u32[]{:S(2)}) collective-permute-start(bf16[2,512,1024]{2,1,0:T(8,128)(2,1)} %param.7), channel_id=1, source_target_pairs={{1,0},{2,1},{3,2},{4,3},{5,4},{6,5},{7,6},{8,7},{9,8},{10,9},{11,1... | collective-permute-start | bytes 6291464 | tf_op jit(solution)/shard_map/ppermute | solution.py:30
  10.2 4.0 %collective-permute-start.3 = (bf16[2,512,1024]{2,1,0:T(8,128)(2,1)}, bf16[2,512,1024]{2,1,0:T(8,128)(2,1)}, u32[]{:S(2)}, u32[]{:S(2)}) collective-permute-start(bf16[2,512,1024]{2,1,0:T(8,128)(2,1)} %param.7), channel_id=1, source_target_pairs={{2,0},{3,1},{4,2},{5,3},{6,4},{7,5},{8,6},{9,7},{10,8},{11,9},{12,... | collective-permute-start | bytes 6291464 | tf_op jit(solution)/shard_map/ppermute | solution.py:17
  14.3 2.5 copy.16
  16.7 0.7 broadcast_subtract_fusion
  17.4 120.2 %collective-permute-done = bf16[2,512,1024]{2,1,0:T(8,128)(2,1)} collective-permute-done((bf16[2,512,1024]{2,1,0:T(8,128)(2,1)}, bf16[2,512,1024]{2,1,0:T(8,128)(2,1)}, u32[]{:S(2)}, u32[]{:S(2)}) %collective-permute-start) | collective-permute-done | bytes 2097184 | tf_op jit(solution)/shard_map/ppermute | solution.py:17
  137.7 3.1 constant_dynamic-update-slice_fusion.5
  140.8 44.8 %collective-permute-done.1 = bf16[2,512,1024]{2,1,0:T(8,128)(2,1)} collective-permute-done((bf16[2,512,1024]{2,1,0:T(8,128)(2,1)}, bf16[2,512,1024]{2,1,0:T(8,128)(2,1)}, u32[]{:S(2)}, u32[]{:S(2)}) %collective-permute-start.1) | collective-permute-done | bytes 2097184 | tf_op jit(solution)/shard_map/ppermute | solution.py:28
  185.6 3.1 constant_dynamic-update-slice_fusion.4
  188.7 0.0 copy-done.1
  188.7 1.6 constant_dynamic-update-slice_fusion.3
  190.3 37.2 %collective-permute-done.2 = bf16[2,512,1024]{2,1,0:T(8,128)(2,1)} collective-permute-done((bf16[2,512,1024]{2,1,0:T(8,128)(2,1)}, bf16[2,512,1024]{2,1,0:T(8,128)(2,1)}, u32[]{:S(2)}, u32[]{:S(2)}) %collective-permute-start.2) | collective-permute-done | bytes 2097184 | tf_op jit(solution)/shard_map/ppermute | solution.py:30
  227.5 3.0 constant_dynamic-update-slice_fusion.2
  230.6 41.9 %collective-permute-done.3 = bf16[2,512,1024]{2,1,0:T(8,128)(2,1)} collective-permute-done((bf16[2,512,1024]{2,1,0:T(8,128)(2,1)}, bf16[2,512,1024]{2,1,0:T(8,128)(2,1)}, u32[]{:S(2)}, u32[]{:S(2)}) %collective-permute-start.3) | collective-permute-done | bytes 2097184 | tf_op jit(solution)/shard_map/ppermute | solution.py:17
  272.5 3.1 constant_dynamic-update-slice_fusion.1
  275.6 10.5 %slice_bitcast_fusion = (bf16[320,8,8,128]{3,1,2,0:T(8,128)(2,1)}, bf16[320,8,8,128]{3,1,2,0:T(8,128)(2,1)}) fusion(bf16[2,2560,1024]{2,1,0:T(8,128)(2,1)} %constant_dynamic-update-slice_fusion.1), kind=kLoop, calls=%fused_computation.36 | loop fusion | bytes 20971520
  286.1 6.4 %copy.15 = bf16[320,8,8,128]{3,2,1,0:T(8,128)(2,1)} copy(bf16[320,8,8,128]{3,1,2,0:T(8,128)(2,1)} %get-tuple-element.120) | data formatting | bytes 10485760
  292.5 3.7 copy.17
  296.3 81.8 %while.12 = (s32[]{:T(128)}, bf16[4,128,1024]{2,1,0:T(8,128)(2,1)}, s32[4,12]{1,0:T(4,128)S(1)}, bf16[20,128,8,128]{3,2,1,0:T(8,128)(2,1)}, s32[4]{0:T(128)S(1)}...) while((s32[]{:T(128)}, bf16[4,128,1024]{2,1,0:T(8,128)(2,1)}, ...), condition=%wide.region_3.4_spmd, body=%wide.region_0.3_spmd.sunk | while | flops 822882816 | bytes 65043320 | solution.py:82
  296.3 3.6 gather_fusion
  299.9 0.6 dynamic_slice.34
  300.5 0.6 fusion.44
  301.1 1.0 constant_dynamic-slice_fusion.3
  302.1 1.4 fusion.46
  303.5 2.6 copy-done
  306.1 1.3 fusion.47
  307.5 3.6 gather_fusion.1
  311.1 4.7 %fusion.48 = bf16[128,8,128]{0,2,1:T(8,128)(2,1)S(1)} fusion(f32[8,128,1536]{2,1,0:T(8,128)} %copy-done, f32[8,128]{1,0:T(8,128)S(1)} %get-tuple-element.167, pred[1536]{0:T(1024)(128)(4,1)S(1)} %fusion.44, bf16[1536,8,128]{2,1,0:T(8,128)(2,1)S(1)} %bitcast.59, f32[128,8]{0,1:T(8,128)S(1)} %bitcast.65), kind=kOutput, calls=%fused_computation.17.clone.1 | convolution fusion | flops 409206784 | bytes 9709056 | tf_op jit(solution)/shard_map/while/body/eval_jaxpr/hqk,khd->qhd/dot_general | solution.py:52
  315.8 0.1 copy.41
  316.0 0.7 constant_dynamic-update-slice_fusion.7
  316.7 3.6 gather_fusion
  320.4 0.6 dynamic_slice.34
  321.0 0.6 fusion.44
  321.5 1.0 constant_dynamic-slice_fusion.3
  322.5 1.4 fusion.46
  324.0 2.6 copy-done
  326.6 1.3 fusion.47
  327.9 3.6 gather_fusion.1
  331.6 4.7 %fusion.48 = bf16[128,8,128]{0,2,1:T(8,128)(2,1)S(1)} fusion(f32[8,128,1536]{2,1,0:T(8,128)} %copy-done, f32[8,128]{1,0:T(8,128)S(1)} %get-tuple-element.167, pred[1536]{0:T(1024)(128)(4,1)S(1)} %fusion.44, bf16[1536,8,128]{2,1,0:T(8,128)(2,1)S(1)} %bitcast.59, f32[128,8]{0,1:T(8,128)S(1)} %bitcast.65), kind=kOutput, calls=%fused_computation.17.clone.1 | convolution fusion | flops 409206784 | bytes 9709056 | tf_op jit(solution)/shard_map/while/body/eval_jaxpr/hqk,khd->qhd/dot_general | solution.py:52
  336.3 0.1 copy.41
  336.4 0.7 constant_dynamic-update-slice_fusion.7
  337.2 3.6 gather_fusion
  340.8 0.6 dynamic_slice.34
  341.4 0.6 fusion.44
  342.0 1.0 constant_dynamic-slice_fusion.3
  343.0 1.4 fusion.46
  344.4 2.6 copy-done
  347.0 1.3 fusion.47
  348.4 3.6 gather_fusion.1
  352.0 4.7 %fusion.48 = bf16[128,8,128]{0,2,1:T(8,128)(2,1)S(1)} fusion(f32[8,128,1536]{2,1,0:T(8,128)} %copy-done, f32[8,128]{1,0:T(8,128)S(1)} %get-tuple-element.167, pred[1536]{0:T(1024)(128)(4,1)S(1)} %fusion.44, bf16[1536,8,128]{2,1,0:T(8,128)(2,1)S(1)} %bitcast.59, f32[128,8]{0,1:T(8,128)S(1)} %bitcast.65), kind=kOutput, calls=%fused_computation.17.clone.1 | convolution fusion | flops 409206784 | bytes 9709056 | tf_op jit(solution)/shard_map/while/body/eval_jaxpr/hqk,khd->qhd/dot_general | solution.py:52
  356.7 0.1 copy.41
  356.9 0.7 constant_dynamic-update-slice_fusion.7
  357.6 3.6 gather_fusion
  361.3 0.6 dynamic_slice.34
  361.9 0.6 fusion.44
  362.4 1.0 constant_dynamic-slice_fusion.3
  363.4 1.4 fusion.46
  364.9 2.6 copy-done
  367.5 1.3 fusion.47
  368.8 3.6 gather_fusion.1
  372.5 4.7 %fusion.48 = bf16[128,8,128]{0,2,1:T(8,128)(2,1)S(1)} fusion(f32[8,128,1536]{2,1,0:T(8,128)} %copy-done, f32[8,128]{1,0:T(8,128)S(1)} %get-tuple-element.167, pred[1536]{0:T(1024)(128)(4,1)S(1)} %fusion.44, bf16[1536,8,128]{2,1,0:T(8,128)(2,1)S(1)} %bitcast.59, f32[128,8]{0,1:T(8,128)S(1)} %bitcast.65), kind=kOutput, calls=%fused_computation.17.clone.1 | convolution fusion | flops 409206784 | bytes 9709056 | tf_op jit(solution)/shard_map/while/body/eval_jaxpr/hqk,khd->qhd/dot_general | solution.py:52
  377.2 0.1 copy.41
  377.3 0.7 constant_dynamic-update-slice_fusion.7
  (21 shorter events, 0.1 us)
Async XLA Ops:
  0.0 188.7 %copy-start.1 = (bf16[2,512,1024]{2,1,0:T(8,128)(2,1)S(1)}, bf16[2,512,1024]{2,1,0:T(8,128)(2,1)}, u32[]{:S(2)}) copy-start(bf16[2,512,1024]{2,1,0:T(8,128)(2,1)} %param.7) | copy-start | bytes 6291460
  0.0 137.7 %collective-permute-start = (bf16[2,512,1024]{2,1,0:T(8,128)(2,1)}, bf16[2,512,1024]{2,1,0:T(8,128)(2,1)}, u32[]{:S(2)}, u32[]{:S(2)}) collective-permute-start(bf16[2,512,1024]{2,1,0:T(8,128)(2,1)} %param.7), channel_id=1, source_target_pairs={{0,2},{1,3},{2,4},{3,5},{4,6},{5,7},{6,8},{7,9},{8,10},{9,11},{10,... | collective-permute-start | bytes 6291464 | tf_op jit(solution)/shard_map/ppermute | solution.py:17
  2.1 183.5 %collective-permute-start.1 = (bf16[2,512,1024]{2,1,0:T(8,128)(2,1)}, bf16[2,512,1024]{2,1,0:T(8,128)(2,1)}, u32[]{:S(2)}, u32[]{:S(2)}) collective-permute-start(bf16[2,512,1024]{2,1,0:T(8,128)(2,1)} %param.7), channel_id=1, source_target_pairs={{0,1},{1,2},{2,3},{3,4},{4,5},{5,6},{6,7},{7,8},{8,9},{9,10},{10,1... | collective-permute-start | bytes 6291464 | tf_op jit(solution)/shard_map/ppermute | solution.py:28
  5.5 222.0 %collective-permute-start.2 = (bf16[2,512,1024]{2,1,0:T(8,128)(2,1)}, bf16[2,512,1024]{2,1,0:T(8,128)(2,1)}, u32[]{:S(2)}, u32[]{:S(2)}) collective-permute-start(bf16[2,512,1024]{2,1,0:T(8,128)(2,1)} %param.7), channel_id=1, source_target_pairs={{1,0},{2,1},{3,2},{4,3},{5,4},{6,5},{7,6},{8,7},{9,8},{10,9},{11,1... | collective-permute-start | bytes 6291464 | tf_op jit(solution)/shard_map/ppermute | solution.py:30
  10.2 262.3 %collective-permute-start.3 = (bf16[2,512,1024]{2,1,0:T(8,128)(2,1)}, bf16[2,512,1024]{2,1,0:T(8,128)(2,1)}, u32[]{:S(2)}, u32[]{:S(2)}) collective-permute-start(bf16[2,512,1024]{2,1,0:T(8,128)(2,1)} %param.7), channel_id=1, source_target_pairs={{2,0},{3,1},{4,2},{5,3},{6,4},{7,5},{8,6},{9,7},{10,8},{11,9},{12,... | collective-permute-start | bytes 6291464 | tf_op jit(solution)/shard_map/ppermute | solution.py:17
  286.1 6.4 %slice-start = ((s8[5242880]{0:T(1024)(128)(4,1)}), s8[4194304]{0:T(1024)(128)(4,1)S(1)}, s32[]{:S(2)}) async-start(s8[5242880]{0:T(1024)(128)(4,1)} %bitcast.60), calls=%async_computation | async-start | bytes 8388608
  286.1 6.4 %slice-start.1 = ((s8[5242880]{0:T(1024)(128)(4,1)}), s8[1048576]{0:T(1024)(128)(4,1)S(1)}, s32[]{:S(2)}) async-start(s8[5242880]{0:T(1024)(128)(4,1)} %bitcast.60), calls=%async_computation.1 | async-start | bytes 2097152
  292.5 3.8 copy-start.2
  303.5 2.6 copy-start
  324.0 2.6 copy-start
  344.4 2.6 copy-start
  364.8 2.6 copy-start
where the time goes:
time: 384 us; the launch traced here: 378 us
  waiting for transfers between devices  244 us (64%)
  local copies, waits for them, and re-layouts  86.4 us (22%)
  matrix products  24.6 us (6%)
  starting transfers between devices  14.2 us (4%)
  other arithmetic  8.39 us (2%)
    ppermute x2, waiting for transfers between devices, from_behind(): return lax.ppermute(block, axis, route)  162 us
    ppermute x1, waiting for transfers between devices, padded(): lax.ppermute(tail, axis, [(i, (i + 1) % count) for i in range(ends)])  44.8 us
    ppermute x1, waiting for transfers between devices, padded(): lax.ppermute(head, axis, [((i + 1) % count, i) for i in range(ends)])  37.2 us
    unnamed x16, local copies, waits for them, and re-layouts  34 us
    dot_general x4, matrix products, masked_block(): jnp.einsum('hqk,khd->qhd', rounded, value_rows, preferred_element_type=jn...  18.8 us
    gather x4, local copies, waits for them, and re-layouts, masked_block(): value_rows_all[chosen].reshape(list_length * BLOCK, HEADS, HEAD_DIM)  14.6 us
    gather x4, local copies, waits for them, and re-layouts, masked_block(): key_rows_all[chosen].reshape(list_length * BLOCK, HEADS, HEAD_DIM)  14.5 us
    while x8, local copies, waits for them, and re-layouts  10.5 us
  transfers between devices with their start and end apart: 4, of which 4 were waited for; matrix products, arithmetic and copies ran while one was open for 4% of the time, Pallas kernels for 0%

commit v1 on v0

v1 whole, which is shorter than its diff:
```python
from functools import partial

import jax
import jax.numpy as jnp
from jax import lax
from jax.experimental import pallas as pl
from jax.experimental.pallas import tpu as pltpu
from jax.sharding import PartitionSpec as P

HEADS = 8
HEAD_DIM = 128
BLOCK = 128
REACH = 6
MESH = pl.DeviceIdType.MESH


def kernel(seq_size, blk_size, lists, counts, q_hbm, kv_hbm, out, q, win, acc, peak, total, bias,
           local_sem, send_r, recv_r, send_l, recv_l):
    rows = q_hbm.shape[0]
    blocks = rows // BLOCK
    near = rows
    far = (REACH - blocks) * BLOCK
    window = 2 * (near + far) + rows
    own = near + far
    scale = HEAD_DIM ** -0.5
    here = lax.axis_index("seq") * blk_size + lax.axis_index("blk")
    last = seq_size * blk_size - 1
    has_left = here > 0
    has_right = here < last
    left = {"seq": (here - 1) // blk_size, "blk": (here - 1) % blk_size}
    right = {"seq": (here + 1) // blk_size, "blk": (here + 1) % blk_size}

    def remote(src, dst, send, recv, to, i):
        return pltpu.make_async_remote_copy(
            src_ref=src, dst_ref=dst, send_sem=send.at[i], recv_sem=recv.at[i], device_id=to, device_id_type=MESH)

    def strip(ref, start, size):
        return ref.at[:, pl.ds(start, size), :]

    to_right = [
        remote(strip(kv_hbm, rows - far, far), strip(win, own - far, far), send_r, recv_r, right, 0),
        remote(strip(kv_hbm, 0, rows - far), strip(win, far, rows - far), send_r, recv_r, right, 1),
        remote(strip(win, own - far, far), strip(win, 0, far), send_r, recv_r, right, 2),
    ]
    to_left = [
        remote(strip(kv_hbm, 0, far), strip(win, own + rows, far), send_l, recv_l, left, 0),
        remote(strip(kv_hbm, far, rows - far), strip(win, own + rows + far, rows - far), send_l, recv_l, left, 1),
        remote(strip(win, own + rows, far), strip(win, own + 2 * rows, far), send_l, recv_l, left, 2),
    ]
    fetch_q = pltpu.make_async_copy(q_hbm, q, local_sem.at[0])
    fetch_kv = pltpu.make_async_copy(kv_hbm, strip(win, own, rows), local_sem.at[1])
    fetch_q.start()
    fetch_kv.start()

    barrier = pltpu.get_barrier_semaphore()

    @pl.when(has_left)
    def _():
        pl.semaphore_signal(barrier, inc=1, device_id=left, device_id_type=MESH)

    @pl.when(has_right)
    def _():
        pl.semaphore_signal(barrier, inc=1, device_id=right, device_id_type=MESH)

    pl.semaphore_wait(barrier, has_left.astype(jnp.int32) + has_right.astype(jnp.int32))

    @pl.when(has_right)
    def _():
        to_right[0].start()

    @pl.when(has_left)
    def _():
        to_left[0].start()

    @pl.when(has_right)
    def _():
        to_right[1].start()

    @pl.when(has_left)
    def _():
        to_left[1].start()

    @pl.when(here == 0)
    def _():
        win[:, 0:own, :] = jnp.zeros((2, own, win.shape[2]), win.dtype)

    @pl.when(here == 1)
    def _():
        win[:, 0:far, :] = jnp.zeros((2, far, win.shape[2]), win.dtype)

    @pl.when(here == last)
    def _():
        win[:, own + rows:window, :] = jnp.zeros((2, own, win.shape[2]), win.dtype)

    @pl.when(here == last - 1)
    def _():
        win[:, window - far:window, :] = jnp.zeros((2, far, win.shape[2]), win.dtype)

    slot = lax.broadcasted_iota(jnp.int32, (8, window), 1) // BLOCK
    first = here * blocks - own // BLOCK
    for i in range(blocks):
        live = jnp.zeros((8, window), jnp.int32)
        for t in range(lists.shape[1]):
            listed = jnp.where(t < counts[i], lists[i, t] - first, -1)
            live = jnp.where(slot == listed, 1, live)
        bias[i] = jnp.where(live == 1, 0.0, -jnp.inf).astype(jnp.float32)

    def attend(which, start, size, opening=False, closing=False):
        def head(h, carry):
            cols = pl.ds(pl.multiple_of(h * HEAD_DIM, HEAD_DIM), HEAD_DIM)
            keys = win[0, start:start + size, cols]
            values = win[1, start:start + size, cols]
            for i in which:
                mine = slice(i * BLOCK, (i + 1) * BLOCK)
                scores = lax.dot_general(
                    q[mine, cols], keys, (((1,), (1,)), ((), ())), preferred_element_type=jnp.float32)
                scores = scores * scale + bias[i, 0:1, start:start + size]
                top = jnp.max(scores, axis=1, keepdims=True)
                if not opening:
                    before = peak[h, mine, 0:1]
                    top = jnp.maximum(top, before)
                weights = jnp.exp(scores - top)
                added = jnp.sum(weights, axis=1, keepdims=True)
                mixed = jnp.dot(weights.astype(jnp.bfloat16), values, preferred_element_type=jnp.float32)
                if not opening:
                    fade = jnp.exp(before - top)
                    added = total[h, mine, 0:1] * fade + added
                    mixed = acc[mine, cols] * fade + mixed
                if closing:
                    out[mine, cols] = (mixed / added).astype(out.dtype)
                else:
                    peak[h, mine, :] = jnp.broadcast_to(top, (BLOCK, HEAD_DIM))
                    total[h, mine, :] = jnp.broadcast_to(added, (BLOCK, HEAD_DIM))
                    acc[mine, cols] = mixed
            return carry

        lax.fori_loop(0, HEADS, head, 0)

    every = range(blocks)
    fetch_q.wait()
    fetch_kv.wait()
    attend(every, own, rows, opening=True)

    @pl.when(has_left)
    def _():
        to_right[0].wait_recv()

    @pl.when(has_left & has_right)
    def _():
        to_right[2].start()

    @pl.when(has_right)
    def _():
        to_left[0].wait_recv()

    @pl.when(has_left & has_right)
    def _():
        to_left[2].start()

    @pl.when(has_left)
    def _():
        to_right[1].wait_recv()

    attend(every, far, rows)

    @pl.when(has_right)
    def _():
        to_left[1].wait_recv()

    attend(every, own + rows, rows)

    @pl.when(here > 1)
    def _():
        to_right[2].wait_recv()

    attend([i for i in every if i * BLOCK < far], 0, far, closing=True)

    @pl.when(here < last - 1)
    def _():
        to_left[2].wait_recv()

    attend([i for i in every if i * BLOCK >= far], window - far, far, closing=True)

    @pl.when(has_right)
    def _():
        to_right[0].wait_send()
        to_right[1].wait_send()

    @pl.when(has_left)
    def _():
        to_left[0].wait_send()
        to_left[1].wait_send()

    @pl.when(has_left & has_right)
    def _():
        to_right[2].wait_send()
        to_left[2].wait_send()


def on_device(seq_size, blk_size, queries, keyvals, key_lists, live_counts):
    rows, width = queries.shape
    blocks = rows // BLOCK
    assert rows == 2 * (REACH - blocks) * BLOCK
    window = rows + 2 * REACH * BLOCK
    return pl.pallas_call(
        partial(kernel, seq_size, blk_size),
        out_shape=jax.ShapeDtypeStruct((rows, width), queries.dtype),
        in_specs=[
            pl.BlockSpec(memory_space=pltpu.SMEM),
            pl.BlockSpec(memory_space=pltpu.SMEM),
            pl.BlockSpec(memory_space=pl.ANY),
            pl.BlockSpec(memory_space=pl.ANY),
        ],
        out_specs=pl.BlockSpec(memory_space=pltpu.VMEM),
        scratch_shapes=[
            pltpu.VMEM((rows, width), jnp.bfloat16),
            pltpu.VMEM((2, window, width), jnp.bfloat16),
            pltpu.VMEM((rows, width), jnp.float32),
            pltpu.VMEM((HEADS, rows, HEAD_DIM), jnp.float32),
            pltpu.VMEM((HEADS, rows, HEAD_DIM), jnp.float32),
            pltpu.VMEM((blocks, 8, window), jnp.float32),
            pltpu.SemaphoreType.DMA((2,)),
            pltpu.SemaphoreType.DMA((3,)),
            pltpu.SemaphoreType.DMA((3,)),
            pltpu.SemaphoreType.DMA((3,)),
            pltpu.SemaphoreType.DMA((3,)),
        ],
        compiler_params=pltpu.CompilerParams(
            collective_id=0, has_side_effects=True, vmem_limit_bytes=40 * 2**20),
    )(key_lists, live_counts, queries, keyvals)


def solution(mesh):
    return jax.shard_map(
        partial(on_device, mesh.shape["seq"], mesh.shape["blk"]),
        mesh=mesh,
        in_specs=(
            P(("parts", "seq", "blk"), None),
            P(None, ("parts", "seq", "blk"), None),
            P(("parts", "seq", "blk"), None),
            P(("parts", "seq", "blk")),
        ),
        out_specs=P(("parts", "seq", "blk"), None),
        check_vma=False,
    )
```

time: 384 us -> 153 us (0.40); the launches traced: 378 us -> 151 us
  waiting for transfers between devices: 244 us -> 0 us
  Pallas kernels: 0 us -> 146 us
  local copies, waits for them, and re-layouts: 86.4 us -> 5.12 us
  matrix products: 24.6 us -> 0 us
  starting transfers between devices: 14.2 us -> 0 us
  other arithmetic: 8.39 us -> 0 us
    ppermute x4 -> x0, waiting for transfers between devices: 244 us -> none  [the longest x2 162 us: from_behind(): return lax.ppermute(block, axis, route)]
    pallas_call x0 -> x1, Pallas kernels: none -> 146 us  [on_device(): pl.pallas_call(partial(kernel, seq_size, blk_size), out_shape=jax.ShapeDt...]
    gather x8 -> x0, local copies, waits for them, and re-layouts: 29.1 us -> none  [the longest x4 14.6 us: masked_block(): value_rows_all[chosen].reshape(list_length * BLOCK, HEADS, HEAD_DIM)]
    unnamed x16 -> x9, local copies, waits for them, and re-layouts: 34 us -> 5.12 us
    dot_general x8 -> x0, matrix products: 24.6 us -> none  [the longest x4 18.8 us: masked_block(): jnp.einsum('hqk,khd->qhd', rounded, value_rows, preferred_element_type=jn...]
    ppermute x4 -> x0, starting transfers between devices: 14.2 us -> none  [the longest x2 6.06 us: from_behind(): return lax.ppermute(block, axis, route)]
    while x8 -> x0, local copies, waits for them, and re-layouts: 10.5 us -> none
    dynamic_slice x8 -> x0, local copies, waits for them, and re-layouts: 6.21 us -> none  [on_device(): attended = lax.map(attend_block, (query_blocks, local_lists, live_counts))]
  transfers between devices with their start and end apart: 4 -> 0, of which waited for: 4 -> 0; matrix products, arithmetic and copies ran while one was open for 4% -> 0% of each run, Pallas kernels for 0% -> 0%
where the time goes in v1:
time: 153 us; the launch traced here: 151 us
  Pallas kernels  146 us (95%)
  local copies, waits for them, and re-layouts  5.12 us (3%)
    pallas_call x1, Pallas kernels, on_device(): pl.pallas_call(partial(kernel, seq_size, blk_size), out_shape=jax.ShapeDt...  146 us
    unnamed x9, local copies, waits for them, and re-layouts  5.12 us

profile of v1, /device:TPU:16, one launch (start us, length us, event | category | flops | bytes accessed | tf_op | source)
XLA Modules:
  0.0 151.0 jit_solution(8362056102403258168)
XLA Ops:
  0.0 0.0 copy-start
  0.0 1.6 %copy-done = bf16[2,512,1024]{2,1,0:T(8,128)(2,1)S(1)} copy-done((bf16[2,512,1024]{2,1,0:T(8,128)(2,1)S(1)}, bf16[2,512,1024]{2,1,0:T(8,128)(2,1)}, u32[]{:S(2)}) %copy-start) | copy-done | bytes 2097176
  1.6 0.0 copy-start.1
  1.6 1.2 copy-done.1
  2.8 0.0 copy-start.2
  2.8 0.7 copy-done.2
  3.5 0.0 copy-start.3
  3.5 0.7 copy-done.3
  4.2 145.8 %shard_map.46 = bf16[512,1024]{1,0:T(8,128)(2,1)S(1)} custom-call(s32[4,12]{1,0:T(4,128)S(1)} %copy-done.2, s32[4]{0:T(128)S(1)} %copy-done.3, bf16[512,1024]{1,0:T(8,128)(2,1)S(1)} %copy-done.1, bf16[2,512,1024]{2,1,0:T(8,128)(2,1)S(1)} %copy-done), custom_call_target="tpu_custom_call" | custom-call | tf_op jit(solution)/shard_map/pallas_call | solution.py:205
  150.0 1.0 copy.6
Async XLA Ops:
  0.0 1.6 %copy-start = (bf16[2,512,1024]{2,1,0:T(8,128)(2,1)S(1)}, bf16[2,512,1024]{2,1,0:T(8,128)(2,1)}, u32[]{:S(2)}) copy-start(bf16[2,512,1024]{2,1,0:T(8,128)(2,1)} %kv_hbm.1) | copy-start | bytes 6291460
  1.6 1.2 copy-start.1
  2.8 0.7 copy-start.2
  3.5 0.7 copy-start.3

commit v2 on v1

v2 whole, which is shorter than its diff:
```python
from functools import partial

import jax
import jax.numpy as jnp
from jax import lax
from jax.experimental import pallas as pl
from jax.experimental.pallas import tpu as pltpu
from jax.sharding import PartitionSpec as P

HEADS = 8
HEAD_DIM = 128
BLOCK = 128
REACH = 6
MESH = pl.DeviceIdType.MESH


def kernel(seq_size, blk_size, lists, counts, q_hbm, kv_hbm, out, q, win, held, acc, peak, total, bias,
           local_sem, send_r, recv_r, send_l, recv_l, send_h, recv_h):
    rows = q_hbm.shape[0]
    blocks = rows // BLOCK
    far_blocks = REACH - blocks
    far = far_blocks * BLOCK
    near = rows
    window = 2 * (near + far) + rows
    own = near + far
    scale = HEAD_DIM ** -0.5
    seq, blk = lax.axis_index("seq"), lax.axis_index("blk")
    here = seq * blk_size + blk
    last = seq_size * blk_size - 1
    has_left = here > 0
    has_right = here < last
    left = {"seq": (here - 1) // blk_size, "blk": (here - 1) % blk_size}
    right = {"seq": (here + 1) // blk_size, "blk": (here + 1) % blk_size}

    odd = seq % 2 == 1
    low, high = blk == 0, blk == blk_size - 1
    after = odd & (seq < seq_size - 1)
    before = jnp.logical_not(odd) & (seq > 0)
    splits_right, splits_left = after & high, before & low
    relays_right, relays_left = after & low, before & high
    corner = (after | before) & (low | high)
    across = {"seq": seq, "blk": blk_size - 1 - blk}
    over = {"seq": jnp.where(odd, seq + 1, seq - 1), "blk": blk}

    def remote(src, dst, send, recv, to):
        return pltpu.make_async_remote_copy(
            src_ref=src, dst_ref=dst, send_sem=send, recv_sem=recv, device_id=to, device_id_type=MESH)

    def strip(ref, block):
        return ref.at[:, block * BLOCK:(block + 1) * BLOCK, :]

    order_r = list(range(blocks - 1, -1, -1))
    order_l = list(range(blocks))
    to_right, to_left, to_held_r, to_held_l, held_r, held_l = [], [], [], [], [], []
    for i in range(blocks):
        for order, base, send, recv, to, direct, to_held, from_held in (
            (order_r, far_blocks, send_r, recv_r, right, to_right, to_held_r, held_r),
            (order_l, own // BLOCK + blocks, send_l, recv_l, left, to_left, to_held_l, held_l),
        ):
            mine = strip(kv_hbm, order[i])
            there = strip(win, base + order[i])
            direct.append(remote(mine, there, send.at[i], recv.at[i], to))
            if i:
                to_held.append(remote(mine, held.at[i - 1], send.at[i], recv_h.at[i - 1], across))
                from_held.append(remote(held.at[i - 1], there, send_h.at[i - 1], recv.at[i], over))
    for i in range(far_blocks):
        k = blocks + i
        b = far_blocks + order_r[i]
        to_right.append(remote(strip(win, b), strip(win, b - blocks), send_r.at[k], recv_r.at[k], right))
        b = own // BLOCK + blocks + order_l[i]
        to_left.append(remote(strip(win, b), strip(win, b + blocks), send_l.at[k], recv_l.at[k], left))

    barrier = pltpu.get_barrier_semaphore()

    @pl.when(has_left)
    def _():
        pl.semaphore_signal(barrier, inc=1, device_id=left, device_id_type=MESH)

    @pl.when(has_right)
    def _():
        pl.semaphore_signal(barrier, inc=1, device_id=right, device_id_type=MESH)

    @pl.when(corner)
    def _():
        pl.semaphore_signal(barrier, inc=1, device_id=across, device_id_type=MESH)
        pl.semaphore_signal(barrier, inc=1, device_id=over, device_id_type=MESH)

    pl.semaphore_wait(
        barrier, has_left.astype(jnp.int32) + has_right.astype(jnp.int32) + 2 * corner.astype(jnp.int32))

    for i in range(blocks):
        for exists, splits, direct, to_held in (
            (has_right, splits_right, to_right, to_held_r), (has_left, splits_left, to_left, to_held_l)):
            if i:
                pl.when(splits)(to_held[i - 1].start)
                pl.when(exists & jnp.logical_not(splits))(direct[i].start)
            else:
                pl.when(exists)(direct[i].start)

    fetch_q = pltpu.make_async_copy(q_hbm, q, local_sem.at[0])
    fetch_kv = pltpu.make_async_copy(kv_hbm, win.at[:, own:own + rows, :], local_sem.at[1])
    fetch_q.start()
    fetch_kv.start()

    @pl.when(here == 0)
    def _():
        win[:, 0:own, :] = jnp.zeros((2, own, win.shape[2]), win.dtype)

    @pl.when(here == 1)
    def _():
        win[:, 0:far, :] = jnp.zeros((2, far, win.shape[2]), win.dtype)

    @pl.when(here == last)
    def _():
        win[:, own + rows:window, :] = jnp.zeros((2, own, win.shape[2]), win.dtype)

    @pl.when(here == last - 1)
    def _():
        win[:, window - far:window, :] = jnp.zeros((2, far, win.shape[2]), win.dtype)

    slot = lax.broadcasted_iota(jnp.int32, (8, window), 1) // BLOCK
    first = here * blocks - own // BLOCK
    for i in range(blocks):
        live = jnp.zeros((8, window), jnp.int32)
        for t in range(lists.shape[1]):
            listed = jnp.where(t < counts[i], lists[i, t] - first, -1)
            live = jnp.where(slot == listed, 1, live)
        bias[i] = jnp.where(live == 1, 0.0, -jnp.inf).astype(jnp.float32)

    def attend(which, start, size, opening=False, closing=False):
        def head(h, carry):
            cols = pl.ds(pl.multiple_of(h * HEAD_DIM, HEAD_DIM), HEAD_DIM)
            keys = win[0, start:start + size, cols]
            values = win[1, start:start + size, cols]
            for i in which:
                mine = slice(i * BLOCK, (i + 1) * BLOCK)
                scores = lax.dot_general(
                    q[mine, cols], keys, (((1,), (1,)), ((), ())), preferred_element_type=jnp.float32)
                scores = scores * scale + bias[i, 0:1, start:start + size]
                top = jnp.max(scores, axis=1, keepdims=True)
                if not opening:
                    old = peak[h, mine, 0:1]
                    top = jnp.maximum(top, old)
                weights = jnp.exp(scores - top)
                added = jnp.sum(weights, axis=1, keepdims=True)
                mixed = jnp.dot(weights.astype(jnp.bfloat16), values, preferred_element_type=jnp.float32)
                if not opening:
                    fade = jnp.exp(old - top)
                    added = total[h, mine, 0:1] * fade + added
                    mixed = acc[mine, cols] * fade + mixed
                if closing:
                    out[mine, cols] = (mixed / added).astype(out.dtype)
                else:
                    peak[h, mine, :] = jnp.broadcast_to(top, (BLOCK, HEAD_DIM))
                    total[h, mine, :] = jnp.broadcast_to(added, (BLOCK, HEAD_DIM))
                    acc[mine, cols] = mixed
            return carry

        lax.fori_loop(0, HEADS, head, 0)

    every = range(blocks)
    fetch_q.wait()
    fetch_kv.wait()
    attend(every, own, rows, opening=True)

    def relay(i):
        @pl.when(relays_right)
        def _():
            to_held_r[i].wait_recv()
            held_r[i].start()

        @pl.when(relays_left)
        def _():
            to_held_l[i].wait_recv()
            held_l[i].start()

    for i in range(blocks):
        pl.when(has_left)(to_right[i].wait_recv)
        if i < far_blocks:
            pl.when(has_left & has_right)(to_right[blocks + i].start)
        pl.when(has_right)(to_left[i].wait_recv)
        if i < far_blocks:
            pl.when(has_left & has_right)(to_left[blocks + i].start)
        if i < blocks - 1:
            relay(i)

    attend(every, far, rows)
    attend(every, own + rows, rows)

    for i in range(far_blocks):
        pl.when(here > 1)(to_right[blocks + i].wait_recv)
    attend([i for i in every if i < far_blocks], 0, far, closing=True)

    for i in range(far_blocks):
        pl.when(here < last - 1)(to_left[blocks + i].wait_recv)
    attend([i for i in every if i >= far_blocks], window - far, far, closing=True)

    for i in range(blocks):
        for exists, splits, direct, to_held, relays, from_held in (
            (has_right, splits_right, to_right, to_held_r, relays_right, held_r),
            (has_left, splits_left, to_left, to_held_l, relays_left, held_l)):
            if i:
                pl.when(splits)(to_held[i - 1].wait_send)
                pl.when(exists & jnp.logical_not(splits))(direct[i].wait_send)
                pl.when(relays)(from_held[i - 1].wait_send)
            else:
                pl.when(exists)(direct[i].wait_send)
    for i in range(far_blocks):
        pl.when(has_left & has_right)(to_right[blocks + i].wait_send)
        pl.when(has_left & has_right)(to_left[blocks + i].wait_send)


def on_device(seq_size, blk_size, queries, keyvals, key_lists, live_counts):
    rows, width = queries.shape
    blocks = rows // BLOCK
    assert rows == 2 * (REACH - blocks) * BLOCK
    window = rows + 2 * REACH * BLOCK
    return pl.pallas_call(
        partial(kernel, seq_size, blk_size),
        out_shape=jax.ShapeDtypeStruct((rows, width), queries.dtype),
        in_specs=[
            pl.BlockSpec(memory_space=pltpu.SMEM),
            pl.BlockSpec(memory_space=pltpu.SMEM),
            pl.BlockSpec(memory_space=pl.ANY),
            pl.BlockSpec(memory_space=pl.ANY),
        ],
        out_specs=pl.BlockSpec(memory_space=pltpu.VMEM),
        scratch_shapes=[
            pltpu.VMEM((rows, width), jnp.bfloat16),
            pltpu.VMEM((2, window, width), jnp.bfloat16),
            pltpu.VMEM((blocks - 1, 2, BLOCK, width), jnp.bfloat16),
            pltpu.VMEM((rows, width), jnp.float32),
            pltpu.VMEM((HEADS, rows, HEAD_DIM), jnp.float32),
            pltpu.VMEM((HEADS, rows, HEAD_DIM), jnp.float32),
            pltpu.VMEM((blocks, 8, window), jnp.float32),
            pltpu.SemaphoreType.DMA((2,)),
            pltpu.SemaphoreType.DMA((REACH,)),
            pltpu.SemaphoreType.DMA((REACH,)),
            pltpu.SemaphoreType.DMA((REACH,)),
            pltpu.SemaphoreType.DMA((REACH,)),
            pltpu.SemaphoreType.DMA((blocks - 1,)),
            pltpu.SemaphoreType.DMA((blocks - 1,)),
        ],
        compiler_params=pltpu.CompilerParams(
            collective_id=0, has_side_effects=True, vmem_limit_bytes=60 * 2**20),
    )(key_lists, live_counts, queries, keyvals)


def solution(mesh):
    return jax.shard_map(
        partial(on_device, mesh.shape["seq"], mesh.shape["blk"]),
        mesh=mesh,
        in_specs=(
            P(("parts", "seq", "blk"), None),
            P(None, ("parts", "seq", "blk"), None),
            P(("parts", "seq", "blk"), None),
            P(("parts", "seq", "blk")),
        ),
        out_specs=P(("parts", "seq", "blk"), None),
        check_vma=False,
    )
```

time: 153 us -> 152 us (level)
  local copies, waits for them, and re-layouts: 5.12 us -> 2.26 us
    unnamed x9 -> x1, local copies, waits for them, and re-layouts: 5.12 us -> 2.26 us
where the time goes in v2:
time: 152 us; the launch traced here: 149 us
  Pallas kernels  147 us (97%)
  local copies, waits for them, and re-layouts  2.26 us (1%)
    pallas_call x1, Pallas kernels, on_device(): pl.pallas_call(partial(kernel, seq_size, blk_size), out_shape=jax.ShapeDt...  147 us

profile of v2, /device:TPU:16, one launch (start us, length us, event | category | flops | bytes accessed | tf_op | source)
XLA Modules:
  0.0 149.2 jit_solution(8894360168018407956)
XLA Ops:
  0.0 147.0 %shard_map.46 = bf16[512,1024]{1,0:T(8,128)(2,1)} custom-call(s32[4,12]{1,0:T(4,128)} %lists.1, s32[4]{0:T(128)} %counts.1, bf16[512,1024]{1,0:T(8,128)(2,1)} %q_hbm.1, bf16[2,512,1024]{2,1,0:T(8,128)(2,1)} %kv_hbm.1), custom_call_target="tpu_custom_call" | custom-call | tf_op jit(solution)/shard_map/pallas_call | solution.py:218
  147.0 2.3 %copy.6 = bf16[512,1024]{1,0:T(8,128)(2,1)} copy(bf16[512,1024]{1,0:T(8,128)(2,1)} %shard_map.46) | data formatting | bytes 2097152

commit v3 on v2

--- a/solution.py
+++ b/solution.py
@@ -37,7 +37,7 @@
     after = odd & (seq < seq_size - 1)
     before = jnp.logical_not(odd) & (seq > 0)
     splits_right, splits_left = after & high, before & low
-    relays_right, relays_left = after & low, before & high
+    relays_right, relays_left = before & high, after & low
     corner = (after | before) & (low | high)
     across = {"seq": seq, "blk": blk_size - 1 - blk}
     over = {"seq": jnp.where(odd, seq + 1, seq - 1), "blk": blk}
@@ -61,8 +61,8 @@
             there = strip(win, base + order[i])
             direct.append(remote(mine, there, send.at[i], recv.at[i], to))
             if i:
-                to_held.append(remote(mine, held.at[i - 1], send.at[i], recv_h.at[i - 1], across))
-                from_held.append(remote(held.at[i - 1], there, send_h.at[i - 1], recv.at[i], over))
+                to_held.append(remote(mine, held.at[i - 1], send.at[i], recv_h.at[i - 1], over))
+                from_held.append(remote(held.at[i - 1], there, send_h.at[i - 1], recv.at[i], across))
     for i in range(far_blocks):
         k = blocks + i
         b = far_blocks + order_r[i]

time: 152 us -> 155 us (1.020)
  the two profiles are of different devices: /device:TPU:16 before, /device:TPU:2 now
where the time goes in v3:
time: 155 us; the launch traced here: 154 us
  Pallas kernels  152 us (98%)
  local copies, waits for them, and re-layouts  2.26 us (1%)
    pallas_call x1, Pallas kernels, on_device(): pl.pallas_call(partial(kernel, seq_size, blk_size), out_shape=jax.ShapeDt...  152 us

profile of v3, /device:TPU:2, one launch (start us, length us, event | category | flops | bytes accessed | tf_op | source)
XLA Modules:
  0.0 154.3 jit_solution(7285657942274394721)
XLA Ops:
  0.0 152.1 %shard_map.46 = bf16[512,1024]{1,0:T(8,128)(2,1)} custom-call(s32[4,12]{1,0:T(4,128)} %lists.1, s32[4]{0:T(128)} %counts.1, bf16[512,1024]{1,0:T(8,128)(2,1)} %q_hbm.1, bf16[2,512,1024]{2,1,0:T(8,128)(2,1)} %kv_hbm.1), custom_call_target="tpu_custom_call" | custom-call | tf_op jit(solution)/shard_map/pallas_call | solution.py:218
  152.1 2.3 %copy.6 = bf16[512,1024]{1,0:T(8,128)(2,1)} copy(bf16[512,1024]{1,0:T(8,128)(2,1)} %shard_map.46) | data formatting | bytes 2097152

commit v4 on v3

--- a/solution.py
+++ b/solution.py
@@ -174,6 +174,9 @@
             to_held_l[i].wait_recv()
             held_l[i].start()
 
+    for i in range(blocks - 1):
+        relay(i)
+
     for i in range(blocks):
         pl.when(has_left)(to_right[i].wait_recv)
         if i < far_blocks:
@@ -181,8 +184,6 @@
         pl.when(has_right)(to_left[i].wait_recv)
         if i < far_blocks:
             pl.when(has_left & has_right)(to_left[blocks + i].start)
-        if i < blocks - 1:
-            relay(i)
 
     attend(every, far, rows)
     attend(every, own + rows, rows)

time: 155 us -> 138 us (0.89)
  the two profiles are of different devices: /device:TPU:2 before, /device:TPU:16 now
where the time goes in v4:
time: 138 us
  Pallas kernels  136 us (99%)
  local copies, waits for them, and re-layouts  2.26 us (2%)
    pallas_call x1, Pallas kernels, on_device(): pl.pallas_call(partial(kernel, seq_size, blk_size), out_shape=jax.ShapeDt...  136 us

profile of v4, /device:TPU:16, one launch (start us, length us, event | category | flops | bytes accessed | tf_op | source)
XLA Modules:
  0.0 137.9 jit_solution(10419914691177927527)
XLA Ops:
  0.0 135.6 %shard_map.46 = bf16[512,1024]{1,0:T(8,128)(2,1)} custom-call(s32[4,12]{1,0:T(4,128)} %lists.1, s32[4]{0:T(128)} %counts.1, bf16[512,1024]{1,0:T(8,128)(2,1)} %q_hbm.1, bf16[2,512,1024]{2,1,0:T(8,128)(2,1)} %kv_hbm.1), custom_call_target="tpu_custom_call" | custom-call | tf_op jit(solution)/shard_map/pallas_call | solution.py:219
  135.6 2.3 %copy.6 = bf16[512,1024]{1,0:T(8,128)(2,1)} copy(bf16[512,1024]{1,0:T(8,128)(2,1)} %shard_map.46) | data formatting | bytes 2097152

commit v5 on v4

--- a/solution.py
+++ b/solution.py
@@ -32,15 +32,13 @@
     left = {"seq": (here - 1) // blk_size, "blk": (here - 1) % blk_size}
     right = {"seq": (here + 1) // blk_size, "blk": (here + 1) % blk_size}
 
-    odd = seq % 2 == 1
+    place = seq % 4 if seq_size % 4 == 0 else seq * 0 - 1
     low, high = blk == 0, blk == blk_size - 1
-    after = odd & (seq < seq_size - 1)
-    before = jnp.logical_not(odd) & (seq > 0)
-    splits_right, splits_left = after & high, before & low
-    relays_right, relays_left = before & high, after & low
-    corner = (after | before) & (low | high)
-    across = {"seq": seq, "blk": blk_size - 1 - blk}
-    over = {"seq": jnp.where(odd, seq + 1, seq - 1), "blk": blk}
+    splits_right, splits_left = (place == 1) & high, (place == 2) & low
+    relays_right, relays_left = (place == 3) & high, (place == 0) & low
+    corner = splits_right | splits_left | relays_right | relays_left
+    over = {"seq": jnp.where(place < 2, seq + 2, seq - 2), "blk": blk}
+    across = {"seq": jnp.where(seq % 2 == 0, seq + 1, seq - 1), "blk": blk_size - 1 - blk}
 
     def remote(src, dst, send, recv, to):
         return pltpu.make_async_remote_copy(
@@ -128,6 +126,9 @@
         bias[i] = jnp.where(live == 1, 0.0, -jnp.inf).astype(jnp.float32)
 
     def attend(which, start, size, opening=False, closing=False):
+        if not which:
+            return
+
         def head(h, carry):
             cols = pl.ds(pl.multiple_of(h * HEAD_DIM, HEAD_DIM), HEAD_DIM)
             keys = win[0, start:start + size, cols]
@@ -189,12 +190,14 @@
     attend(every, own + rows, rows)
 
     for i in range(far_blocks):
+        furthest = far_blocks - 1 - i
         pl.when(here > 1)(to_right[blocks + i].wait_recv)
-    attend([i for i in every if i < far_blocks], 0, far, closing=True)
-
-    for i in range(far_blocks):
+        attend(range(furthest), furthest * BLOCK, BLOCK)
+        attend([furthest], furthest * BLOCK, BLOCK, closing=True)
+        furthest = window // BLOCK - far_blocks + i
         pl.when(here < last - 1)(to_left[blocks + i].wait_recv)
-    attend([i for i in every if i >= far_blocks], window - far, far, closing=True)
+        attend([blocks - far_blocks + i], furthest * BLOCK, BLOCK, closing=True)
+        attend(range(blocks - far_blocks + i + 1, blocks), furthest * BLOCK, BLOCK)
 
     for i in range(blocks):
         for exists, splits, direct, to_held, relays, from_held in (

time: 138 us -> 148 us (1.072); the launches traced: 138 us -> 146 us
  Pallas kernels: 136 us -> 144 us
    pallas_call x1, Pallas kernels: 136 us -> 144 us  [on_device(): pl.pallas_call(partial(kernel, seq_size, blk_size), out_shape=jax.ShapeDt...]
where the time goes in v5:
time: 148 us; the launch traced here: 146 us
  Pallas kernels  144 us (97%)
  local copies, waits for them, and re-layouts  2.26 us (2%)
    pallas_call x1, Pallas kernels, on_device(): pl.pallas_call(partial(kernel, seq_size, blk_size), out_shape=jax.ShapeDt...  144 us

profile of v5, /device:TPU:16, one launch (start us, length us, event | category | flops | bytes accessed | tf_op | source)
XLA Modules:
  0.0 146.1 jit_solution(3430975420641486957)
XLA Ops:
  0.0 143.9 %shard_map.46 = bf16[512,1024]{1,0:T(8,128)(2,1)} custom-call(s32[4,12]{1,0:T(4,128)} %lists.1, s32[4]{0:T(128)} %counts.1, bf16[512,1024]{1,0:T(8,128)(2,1)} %q_hbm.1, bf16[2,512,1024]{2,1,0:T(8,128)(2,1)} %kv_hbm.1), custom_call_target="tpu_custom_call" | custom-call | tf_op jit(solution)/shard_map/pallas_call | solution.py:222
  143.9 2.3 %copy.6 = bf16[512,1024]{1,0:T(8,128)(2,1)} copy(bf16[512,1024]{1,0:T(8,128)(2,1)} %shard_map.46) | data formatting | bytes 2097152

commit v6 on v4

--- a/solution.py
+++ b/solution.py
@@ -128,6 +128,9 @@
         bias[i] = jnp.where(live == 1, 0.0, -jnp.inf).astype(jnp.float32)
 
     def attend(which, start, size, opening=False, closing=False):
+        if not which:
+            return
+
         def head(h, carry):
             cols = pl.ds(pl.multiple_of(h * HEAD_DIM, HEAD_DIM), HEAD_DIM)
             keys = win[0, start:start + size, cols]
@@ -189,12 +192,14 @@
     attend(every, own + rows, rows)
 
     for i in range(far_blocks):
+        furthest = far_blocks - 1 - i
         pl.when(here > 1)(to_right[blocks + i].wait_recv)
-    attend([i for i in every if i < far_blocks], 0, far, closing=True)
-
-    for i in range(far_blocks):
+        attend(range(furthest), furthest * BLOCK, BLOCK)
+        attend([furthest], furthest * BLOCK, BLOCK, closing=True)
+        furthest = window // BLOCK - far_blocks + i
         pl.when(here < last - 1)(to_left[blocks + i].wait_recv)
-    attend([i for i in every if i >= far_blocks], window - far, far, closing=True)
+        attend([blocks - far_blocks + i], furthest * BLOCK, BLOCK, closing=True)
+        attend(range(blocks - far_blocks + i + 1, blocks), furthest * BLOCK, BLOCK)
 
     for i in range(blocks):
         for exists, splits, direct, to_held, relays, from_held in (

time: 138 us -> 147 us (1.065)
  Pallas kernels: 136 us -> 144 us
    pallas_call x1, Pallas kernels: 136 us -> 144 us  [on_device(): pl.pallas_call(partial(kernel, seq_size, blk_size), out_shape=jax.ShapeDt...]
where the time goes in v6:
time: 147 us; the launch traced here: 146 us
  Pallas kernels  144 us (98%)
  local copies, waits for them, and re-layouts  2.26 us (2%)
    pallas_call x1, Pallas kernels, on_device(): pl.pallas_call(partial(kernel, seq_size, blk_size), out_shape=jax.ShapeDt...  144 us

profile of v6, /device:TPU:16, one launch (start us, length us, event | category | flops | bytes accessed | tf_op | source)
XLA Modules:
  0.0 145.8 jit_solution(1395903949752160826)
XLA Ops:
  0.0 143.6 %shard_map.46 = bf16[512,1024]{1,0:T(8,128)(2,1)} custom-call(s32[4,12]{1,0:T(4,128)} %lists.1, s32[4]{0:T(128)} %counts.1, bf16[512,1024]{1,0:T(8,128)(2,1)} %q_hbm.1, bf16[2,512,1024]{2,1,0:T(8,128)(2,1)} %kv_hbm.1), custom_call_target="tpu_custom_call" | custom-call | tf_op jit(solution)/shard_map/pallas_call | solution.py:224
  143.6 2.3 %copy.6 = bf16[512,1024]{1,0:T(8,128)(2,1)} copy(bf16[512,1024]{1,0:T(8,128)(2,1)} %shard_map.46) | data formatting | bytes 2097152
